TPU v7x, 256 devices: a whole 4x4x8 slice. The times are simulated.
256 devices in a mesh: chan: 32 (over y, z_lo, core), win: 8 (over x, z_hi).
Axes of the slice: x: 4, y: 4, z: 8 (z_hi: 2, z_lo: 4; z = z_hi * 4 + z_lo), core: 2. Of those that a mesh axis runs over, the one named last changes fastest.
Arguments:
- record: float32 [4096, 12288], P('chan', 'win')
- owners: int32 [3], replicated, may hold values from 0 to 31, as said below
- pair_mask: int32 [32, 32], replicated, may hold values from 0 to 1, as said below
Outputs:
- correlations: float32 [3, 81, 128, 4096], P(None, None, 'win', 'chan')
Inputs may be any that keep to these rules, and one draw needn't show every extreme that they name: `owners`: 3 different channel blocks. pair_mask[o, b] is 0 wherever b < o.
All inputs are finite; a program needn't handle non-finite values.
Results may differ from a plain program's by a relative error of at most 0.0041.
Values may be sent and summed in bfloat16 or wider, within the bound.
No kernel may reach another device: no remote copies, remote signals or barrier semaphores. Data moves between devices by JAX's collectives and lax.ppermute only.
A program may use at most 128 MiB of HBM per device.

v0:
```python
import math

import jax
import jax.numpy as jnp
from jax import lax
from jax.sharding import PartitionSpec as P

LAG = 40
STEPS = 3


def spread(shard, axis, root):
    mine = lax.axis_index(axis) == root
    return lax.psum(jnp.where(mine, shard, jnp.zeros_like(shard)), axis)


def lagged_products(anchor, sliding, length):
    lag_count = 2 * LAG + 1

    def lag_turn(state, lag_group):
        pieces = []
        for offset in range(9):
            lag_index = lag_group * 9 + offset
            start_at = 2 * LAG - lag_index
            pieces.append(lax.dynamic_slice_in_dim(sliding, start_at, length, 1))
        shifted = jnp.stack(pieces)
        product = jnp.einsum("gct,dt->gcd", shifted, anchor, preferred_element_type=jnp.float32)
        return (state, product)

    _, stacked = lax.scan(lag_turn, None, jnp.arange(lag_count // 9, dtype=jnp.int32))
    return stacked.reshape((lag_count,) + stacked.shape[2:])


def local(record, owners, pair_mask):
    row_count, span_len = record.shape
    total_channels = row_count * lax.axis_size("chan")
    total_time = span_len * lax.axis_size("win")
    lag_count = 2 * LAG + 1
    common = lax.psum(jnp.sum(record, axis=0), "chan") / total_channels
    cleaned = record - common[None, :]
    power = lax.psum(jnp.sum(cleaned * cleaned, axis=1), "win") / total_time
    whitened = (cleaned / jnp.sqrt(power + 1e-06)[:, None]).astype(jnp.bfloat16)
    own_block = lax.axis_index("chan")
    win_piece = lax.axis_index("win")
    row_share = row_count // lax.axis_size("win")
    norm_scale = 1.0 / math.sqrt(total_time)
    results = []
    full_record = lax.all_gather(whitened, "win", axis=1, tiled=True)
    for step_index in range(STEPS):
        owner_id = owners[step_index]
        source_all = spread(full_record, "chan", owner_id)
        own_rows = lax.dynamic_slice_in_dim(source_all, win_piece * row_share, row_share, 0)
        source_pad = jnp.pad(own_rows, ((0, 0), (LAG, LAG)))
        pair_flag = pair_mask[owner_id, own_block]
        partial_value = lax.cond(
            pair_flag > 0,
            lambda: lagged_products(full_record, source_pad, total_time),
            lambda: jnp.zeros((lag_count, row_share, row_count), jnp.float32),
        )
        results.append(partial_value * norm_scale)
    return jnp.stack(results)


def solution(mesh):
    in_specs = (P("chan", "win"), P(), P())
    out_specs = P(None, None, "win", "chan")
    return jax.shard_map(local, mesh=mesh, in_specs=in_specs, out_specs=out_specs, check_vma=False)
```

profile of v0, /device:TPU:127, one launch (start us, length us, event | category | flops | bytes accessed | tf_op | source)
XLA Modules:
  0.0 665.5 jit_solution(17046286345961294877)
XLA Ops:
  7.7 67.8 %psum.35 = f32[1536]{0:T(1024)S(1)} all-reduce(f32[1536]{0:T(1024)S(1)} %reduce_sum.18), channel_id=1, replica_groups=mesh['chan'=32,'win'=8] {'chan'}, use_global_device_ids=true, to_apply=%region_1.0 | all-reduce | flops 1536 | bytes 12288 | tf_op jit(solution)/shard_map/psum | solution.py:39
  76.9 24.0 %psum.36 = f32[128]{0:T(128)S(1)} all-reduce(f32[128]{0:T(128)S(1)} %multiply_reduce_fusion), channel_id=1, replica_groups=mesh['chan'=32,'win'=8] {'win'}, use_global_device_ids=true, to_apply=%region_3.0 | all-reduce | flops 128 | bytes 1024 | tf_op jit(solution)/shard_map/psum | solution.py:41
  100.9 2.0 divide_convert_fusion
  106.4 85.2 %all-gather.2.cloned.1.call-done = bf16[128,12288]{1,0:T(8,128)(2,1)} async-done(((bf16[128,1536]{1,0:T(8,128)(2,1)}), bf16[128,12288]{1,0:T(8,128)(2,1)}) %all-gather.2.cloned.1.call-update) | async-done | bytes 3145744 | tf_op jit(solution)/shard_map/all_gather | solution.py:48
  191.6 5.1 broadcast_select_fusion.2
  206.1 309.2 %all-reduce.6.cloned.1.call-done = (bf16[128,12288]{1,0:T(8,128)(2,1)}, bf16[128,12288]{1,0:T(8,128)(2,1)}, bf16[128,12288]{1,0:T(8,128)(2,1)}) async-done(((bf16[128,12288]{1,0:T(8,128)(2,1)}, bf16[128,12288]{1,0:T(8,128)(2,1)}, bf16[128,12288]{1,0:T(8,128)(2,1)}), (bf16[128,12288]{1,0:T(8,128)(2,1)}, bf16[128,12288]{1,0:T(8,128)(2,1)}, bf16[128,12288]{1,0:T(8,128)(2,1)})) %all-reduce.6.cloned.1.call-update) | async-done | bytes 9437200 | tf_op jit(solution)/shard_map/psum | solution.py:14
  515.3 46.6 %conditional.3 = (f32[81,16,128]{2,1,0:T(8,128)}) conditional(s32[]{:T(128)} %bitcast.91, () %tuple.83, (bf16[128,12288]{1,0:T(8,128)(2,1)}, s32[]{:T(128)}, bf16[128,12288]{1,0:T(8,128)(2,1)S(1)}) %tuple.140), branch_computations={%region_5.6_spmd, %region_6.9_spmd} | conditional | flops 452984864 | bytes 15412661 | solution.py:55
  516.7 45.2 %while.42 = (s32[]{:T(128)}, f32[9,9,16,128]{3,2,1,0:T(8,128)}, s32[9]{0:T(128)S(1)}, bf16[16,12368]{1,0:T(8,128)(2,1)S(1)}, bf16[128,12288]{1,0:T(8,128)(2,1)S(...) while((s32[]{:T(128)}, f32[9,9,16,128]{3,2,1,0:T(8,128)}, ...), condition=%wide.region_8.8_spmd, body=%wide.region_7.7_spmd.sunk | while | flops 452984864 | bytes 13837035 | solution.py:30
  519.8 1.9 fusion.46
  524.8 1.9 fusion.46
  529.8 1.9 fusion.46
  534.8 1.9 fusion.46
  539.9 1.9 fusion.46
  544.9 1.9 fusion.46
  549.9 1.9 fusion.46
  554.9 1.9 fusion.46
  560.0 1.9 fusion.46
  561.9 2.0 multiply_bitcast_fusion.2
  563.9 45.4 %conditional.5 = (f32[81,16,128]{2,1,0:T(8,128)}) conditional(s32[]{:T(128)} %bitcast.97, () %tuple.87, (bf16[128,12288]{1,0:T(8,128)(2,1)}, s32[]{:T(128)}, bf16[128,12288]{1,0:T(8,128)(2,1)S(1)}) %tuple.141), branch_computations={%region_15.16_spmd, %region_16.19_spmd} | conditional | flops 452984864 | bytes 15412661 | solution.py:55
  565.3 44.1 %while.44 = (s32[]{:T(128)}, f32[9,9,16,128]{3,2,1,0:T(8,128)}, s32[9]{0:T(128)S(1)}, bf16[16,12368]{1,0:T(8,128)(2,1)S(1)}, bf16[128,12288]{1,0:T(8,128)(2,1)S(...) while((s32[]{:T(128)}, f32[9,9,16,128]{3,2,1,0:T(8,128)}, ...), condition=%wide.region_18.18_spmd, body=%wide.region_17.17_spmd.sunk | while | flops 452984864 | bytes 13837035 | solution.py:30
  568.2 1.9 fusion.40
  573.1 1.9 fusion.40
  578.0 1.9 fusion.40
  582.9 1.9 fusion.40
  587.8 1.9 fusion.40
  592.7 1.9 fusion.40
  597.6 1.9 fusion.40
  607.4 1.9 fusion.40
  609.3 45.4 %conditional.4 = (f32[81,16,128]{2,1,0:T(8,128)}) conditional(s32[]{:T(128)} %bitcast.94, () %tuple.85, (bf16[128,12288]{1,0:T(8,128)(2,1)}, s32[]{:T(128)}, bf16[128,12288]{1,0:T(8,128)(2,1)S(1)}) %tuple.142), branch_computations={%region_10.11_spmd, %region_11.14_spmd} | conditional | flops 452984864 | bytes 15412661 | solution.py:55
  610.7 44.0 %while.43 = (s32[]{:T(128)}, f32[9,9,16,128]{3,2,1,0:T(8,128)}, s32[9]{0:T(128)S(1)}, bf16[16,12368]{1,0:T(8,128)(2,1)S(1)}, bf16[128,12288]{1,0:T(8,128)(2,1)S(...) while((s32[]{:T(128)}, f32[9,9,16,128]{3,2,1,0:T(8,128)}, ...), condition=%wide.region_13.13_spmd, body=%wide.region_12.12_spmd.sunk | while | flops 452984864 | bytes 13837035 | solution.py:30
  647.9 2.0 fusion.43
  656.1 2.5 pad_maximum_fusion
  (304 shorter events, 89.1 us)
Async XLA Ops:
  6.5 185.0 %all-gather.2.cloned.1.call-start = ((), (), s32[]{:S(2)}) async-start(), calls=%async_computation | async-start | bytes 3538944 | tf_op jit(solution)/shard_map/all_gather | solution.py:48
  103.0 412.3 %all-reduce.6.cloned.1.call-start = ((), (), s32[]{:S(2)}) async-start(), calls=%async_computation.1 | async-start | bytes 18874368 | tf_op jit(solution)/shard_map/psum | solution.py:14
  196.7 318.6 %copy-start = (bf16[128,12288]{1,0:T(8,128)(2,1)S(1)}, bf16[128,12288]{1,0:T(8,128)(2,1)}, u32[]{:S(2)}) copy-start(bf16[128,12288]{1,0:T(8,128)(2,1)} %all-gather.2.cloned.1.call-done) | copy-start | bytes 9437188
Sparse Core Ops, SparseCore 0:
  103.1 88.4 all-gather.1
  196.8 318.4 all-reduce.5
where the time goes:
time: 666 us; the launch traced here: 665 us
  waiting for transfers between devices  394 us (59%)
  blocking collectives  91.9 us (14%)
  local copies, waits for them, and re-layouts  67.7 us (10%)
  matrix products  52.5 us (8%)
  between operations  23.3 us (3%)
  loops' own time  20.1 us (3%)
  other arithmetic  15.6 us (2%)
    psum x1, waiting for transfers between devices, spread(): return lax.psum(jnp.where(mine, shard, jnp.zeros_like(shard)), axis)  309 us
    all_gather x1, waiting for transfers between devices, local(): full_record = lax.all_gather(whitened, 'win', axis=1, tiled=True)  85.2 us
    psum x1, blocking collectives, local(): common = lax.psum(jnp.sum(record, axis=0), 'chan') / total_channels  67.8 us
    dot_general x27, matrix products, lag_turn(): jnp.einsum('gct,dt->gcd', shifted, anchor, preferred_element_type=jnp.flo...  52.5 us
    while x216, local copies, waits for them, and re-layouts  38.9 us
    psum x1, blocking collectives, local(): power = lax.psum(jnp.sum(cleaned * cleaned, axis=1), 'win') / total_time  24 us
    another operation x3, loops' own time, lagged_products(): lax.scan(lag_turn, None, jnp.arange(lag_count // 9, dtype=jnp.int32))  20 us
    dynamic_slice x27, local copies, waits for them, and re-layouts, lagged_products(): lax.scan(lag_turn, None, jnp.arange(lag_count // 9, dtype=jnp.int32))  17 us
  transfers between devices with their start and end apart: 2, of which 2 were waited for; matrix products, arithmetic and copies ran while one was open for 0% of the time, Pallas kernels for 0%

commit v1 on v0

v1 whole, which is shorter than its diff:
```python
import functools
import math

import jax
import jax.numpy as jnp
from jax import lax
from jax.experimental import pallas as pl
from jax.experimental.pallas import tpu as pltpu
from jax.sharding import PartitionSpec as P

LAG = 40
STEPS = 3
LAGS = 2 * LAG + 1
HALF = LAG + 1
EDGE = 128


def permute(value, axis, target):
    size = lax.axis_size(axis)
    return lax.ppermute(value, axis, [(i, target(i)) for i in range(size)])


def core_flip(i):
    return i ^ 1


def z_shift(d):
    return lambda i: (i & ~6) | ((((i >> 1) + d) & 3) << 1)


def y_shift(d):
    return lambda i: (i & 7) | ((((i >> 3) + d) & 3) << 3)


def hi_flip(i):
    return i ^ 1


def x_shift(d):
    return lambda i: (i & 1) | ((((i >> 1) + d) & 3) << 1)


def correlate_kernel(index_ref, *refs, span, chunk, group):
    own_refs, block_refs = refs[:4], refs[4:12]
    out_ref, own, block, left, right, total = refs[12:]
    rows = own.shape[0]
    share = rows // STEPS
    width = block.shape[0]
    length = block.shape[1] - EDGE
    quarter = span // 4
    bf16 = jnp.bfloat16

    own[:, :EDGE] = jnp.zeros((rows, EDGE), bf16)
    own[:, EDGE + length:] = jnp.zeros((rows, EDGE), bf16)
    block[:, length:] = jnp.zeros((width, EDGE), bf16)
    own_power = jnp.zeros((rows, EDGE), jnp.float32)
    for d in range(4):
        where = index_ref[d]
        for w in range(length // span):
            piece = own_refs[d][:, w * quarter:(w + 1) * quarter]
            start = pl.multiple_of(EDGE + w * span + where * quarter, EDGE)
            own[:, pl.ds(start, quarter)] = piece
            wide = piece.astype(jnp.float32)
            for k in range(quarter // EDGE):
                part = wide[:, k * EDGE:(k + 1) * EDGE]
                own_power += part * part
    block_power = jnp.zeros((width, EDGE), jnp.float32)
    for d in range(8):
        piece = block_refs[d][...]
        start = pl.multiple_of(index_ref[4 + d] * span, EDGE)
        block[:, pl.ds(start, span)] = piece
        wide = piece.astype(jnp.float32)
        for k in range(span // EDGE):
            part = wide[:, k * EDGE:(k + 1) * EDGE]
            block_power += part * part
    own_power = jnp.sum(own_power, axis=1, keepdims=True) / length
    block_power = jnp.sum(block_power, axis=1, keepdims=True) / length
    own_scale = 1.0 / jnp.sqrt(own_power + 1e-06)
    block_scale = 1.0 / jnp.sqrt(block_power + 1e-06)
    block_scale = jnp.transpose(jnp.broadcast_to(block_scale, (width, width)))[:1]

    def product(a, b):
        return lax.dot_general(a, b, (((1,), (1,)), ((), ())), preferred_element_type=jnp.float32)

    lead = own[:, :2 * EDGE]
    for l in range(HALF):
        left[l * rows:(l + 1) * rows, :EDGE] = lead[:, LAG - l:LAG - l + EDGE]
    before = jnp.concatenate([jnp.zeros((width, EDGE - HALF), bf16), block[:, :HALF]], axis=1)
    total[:, :width] = jnp.zeros((HALF * rows, width), jnp.float32)
    total[:, width:] = product(left[:, :EDGE], before)

    def step(k, carry):
        start = pl.multiple_of(k * chunk, EDGE)
        mine = own[:, pl.ds(start + EDGE, chunk + EDGE)]
        theirs = block[:, pl.ds(start, chunk + EDGE)]
        right[:width] = theirs[:, :chunk]
        right[width:] = theirs[:, HALF:HALF + chunk]
        for g in range(0, HALF, group):
            stop = min(g + group, HALF)
            for l in range(g, stop):
                left[l * rows:(l + 1) * rows] = mine[:, LAG - l:LAG - l + chunk]
            part = slice(g * rows, stop * rows)
            total[part] += product(left[part], right[...])
        return carry

    lax.fori_loop(0, length // chunk, step, 0)
    norm = 1.0 / math.sqrt(length)
    for s in range(STEPS):
        flag = index_ref[12 + s].astype(jnp.float32) * norm
        scale = own_scale[s * share:(s + 1) * share] * (block_scale * flag)
        for l in range(HALF):
            at = slice(l * rows + s * share, l * rows + (s + 1) * share)
            out_ref[s, l] = total[at, :width] * scale
            if l + HALF < LAGS:
                out_ref[s, l + HALF] = total[at, width:] * scale


def correlate(index, own, block):
    rows, width, span = own[0].shape[0], block[0].shape[0], block[0].shape[1]
    length = span * len(block)
    chunk = 3072
    vmem = pl.BlockSpec(memory_space=pltpu.VMEM)
    return pl.pallas_call(
        functools.partial(correlate_kernel, span=span, chunk=chunk, group=14),
        out_shape=jax.ShapeDtypeStruct((STEPS, LAGS, rows // STEPS, width), jnp.float32),
        in_specs=[pl.BlockSpec(memory_space=pltpu.SMEM)] + [vmem] * 12,
        out_specs=vmem,
        scratch_shapes=[
            pltpu.VMEM((rows, length + 2 * EDGE), jnp.bfloat16),
            pltpu.VMEM((width, length + EDGE), jnp.bfloat16),
            pltpu.VMEM((HALF * rows, chunk), jnp.bfloat16),
            pltpu.VMEM((2 * width, chunk), jnp.bfloat16),
            pltpu.VMEM((HALF * rows, 2 * width), jnp.float32),
        ],
        compiler_params=pltpu.CompilerParams(vmem_limit_bytes=56 * 2**20),
        cost_estimate=pl.CostEstimate(
            flops=2 * HALF * rows * 2 * width * length, bytes_accessed=6 * 2**20, transcendentals=0
        ),
    )(index, *own, *block)


def local(record, owners, pair_mask):
    width, span = record.shape
    channels = width * lax.axis_size("chan")
    chan, win = lax.axis_index("chan"), lax.axis_index("win")

    sums = jnp.sum(record, axis=0)
    sums = sums + permute(sums, "chan", core_flip)
    sums = sums + (permute(sums, "chan", z_shift(1)) + permute(sums, "chan", z_shift(2)) + permute(sums, "chan", z_shift(3)))
    sums = sums + (permute(sums, "chan", y_shift(1)) + permute(sums, "chan", y_shift(2)) + permute(sums, "chan", y_shift(3)))
    cleaned = (record - (sums / channels)[None, :]).astype(jnp.bfloat16)

    far = permute(cleaned, "win", hi_flip)
    block = [cleaned] + [permute(cleaned, "win", x_shift(d)) for d in (1, 2, 3)]
    block += [far] + [permute(far, "win", x_shift(d)) for d in (1, 2, 3)]

    quarter = span // 4
    pieces = cleaned.reshape(8, 8, 2, 4, quarter).transpose(3, 1, 0, 2, 4).reshape(256, 2, quarter)
    pieces = lax.all_to_all(pieces, ("chan", "win"), 0, 0).reshape(32, 8, 2, quarter)
    mine = jnp.stack([lax.dynamic_index_in_dim(pieces, owners[s], 0, False) for s in range(STEPS)])
    pair = jnp.stack([mine, permute(mine, "chan", core_flip)])
    core = chan & 1
    pair = jnp.where(core == 0, pair, pair[::-1])
    lo = (chan >> 1) & 3
    ring = [pair] + [permute(pair, "chan", z_shift(d)) for d in (1, 2, 3)]
    ring = jnp.stack(ring + ring)
    ring = lax.dynamic_slice_in_dim(ring[::-1], 3 - lo, 4, 0)
    ring = ring.reshape(8, STEPS, 8, 2, quarter).transpose(1, 0, 3, 2, 4).reshape(STEPS * 16, 8 * quarter)
    own = [ring] + [permute(ring, "chan", y_shift(d)) for d in (1, 2, 3)]

    y, x, hi = chan >> 3, win >> 1, win & 1
    index = [(y - d) & 3 for d in range(4)]
    index += [(((x - d) & 3) << 1) | hi for d in range(4)] + [(((x - d) & 3) << 1) | (1 - hi) for d in range(4)]
    index += [pair_mask[owners[s], chan] for s in range(STEPS)]
    index = jnp.stack(index).astype(jnp.int32)
    return correlate(index, own, block)


def solution(mesh):
    in_specs = (P("chan", "win"), P(), P())
    out_specs = P(None, None, "win", "chan")
    return jax.shard_map(local, mesh=mesh, in_specs=in_specs, out_specs=out_specs, check_vma=False)
```

time: 666 us -> 132 us (0.20)
  the two profiles are of different devices: /device:TPU:127 before, /device:TPU:1 now
where the time goes in v1:
time: 132 us
  waiting for transfers between devices  55.5 us (42%)
  starting transfers between devices  39.2 us (30%)
  Pallas kernels  20.9 us (16%)
  local copies, waits for them, and re-layouts  7.81 us (6%)
  between operations  5.66 us (4%)
  other arithmetic  2.45 us (2%)
    ppermute x21, waiting for transfers between devices, permute(): return lax.ppermute(value, axis, [(i, target(i)) for i in range(size)])  43.1 us
    ppermute x21, starting transfers between devices, permute(): return lax.ppermute(value, axis, [(i, target(i)) for i in range(size)])  25.2 us
    pallas_call x1, Pallas kernels, correlate(): pl.pallas_call(functools.partial(correlate_kernel, span=span, chunk=chunk...  20.9 us
    all_to_all x1, starting transfers between devices, local(): lax.all_to_all(pieces, ('chan', 'win'), 0, 0).reshape(32, 8, 2, quarter)  14 us
    all_to_all x1, waiting for transfers between devices, local(): lax.all_to_all(pieces, ('chan', 'win'), 0, 0).reshape(32, 8, 2, quarter)  12.4 us
  transfers between devices with their start and end apart: 22, of which 13 were waited for; matrix products, arithmetic and copies ran while one was open for 4% of the time, Pallas kernels for 0%

profile of v1, /device:TPU:1, one launch (start us, length us, event | category | flops | bytes accessed | tf_op | source)
XLA Modules:
  0.0 131.6 jit_solution(16127936258702617631)
XLA Ops:
  0.0 1.2 reduce_sum.9
  1.2 3.3 %collective-permute-start = (f32[1536]{0:T(1024)S(1)}, f32[1536]{0:T(1024)S(1)}, u32[]{:S(2)}, u32[]{:S(2)}) collective-permute-start(f32[1536]{0:T(1024)S(1)} %reduce_sum.9), channel_id=1, source_target_pairs={{0,8},{8,0},{16,24},{24,16},{32,40},{40,32},{48,56},{56,48},{64,72... | collective-permute-start | bytes 18440 | tf_op jit(solution)/shard_map/ppermute | solution.py:20
  4.5 0.8 collective-permute-done
  5.3 2.6 %collective-permute-start.3 = (f32[1536]{0:T(1024)S(1)}, f32[1536]{0:T(1024)S(1)}, u32[]{:S(2)}, u32[]{:S(2)}) collective-permute-start(f32[1536]{0:T(1024)S(1)} %add.53), channel_id=1, source_target_pairs={{0,48},{8,56},{16,0},{24,8},{32,16},{40,24},{48,32},{56,40},{64,11... | collective-permute-start | bytes 18440 | tf_op jit(solution)/shard_map/ppermute | solution.py:20
  8.8 2.6 %collective-permute-done.2 = f32[1536]{0:T(1024)S(1)} collective-permute-done((f32[1536]{0:T(1024)S(1)}, f32[1536]{0:T(1024)S(1)}, u32[]{:S(2)}, u32[]{:S(2)}) %collective-permute-start.2) | collective-permute-done | bytes 6176 | tf_op jit(solution)/shard_map/ppermute | solution.py:20
  11.4 0.9 collective-permute-done.1
  12.3 2.7 %collective-permute-start.6 = (f32[1536]{0:T(1024)S(1)}, f32[1536]{0:T(1024)S(1)}, u32[]{:S(2)}, u32[]{:S(2)}) collective-permute-start(f32[1536]{0:T(1024)S(1)} %add_add_fusion), channel_id=1, source_target_pairs={{0,192},{8,200},{16,208},{24,216},{32,224},{40,232},{48,240},{56,2... | collective-permute-start | bytes 18440 | tf_op jit(solution)/shard_map/ppermute | solution.py:20
  15.4 0.7 collective-permute-start.4
  16.0 3.0 %collective-permute-done.5 = f32[1536]{0:T(1024)S(1)} collective-permute-done((f32[1536]{0:T(1024)S(1)}, f32[1536]{0:T(1024)S(1)}, u32[]{:S(2)}, u32[]{:S(2)}) %collective-permute-start.5) | collective-permute-done | bytes 6176 | tf_op jit(solution)/shard_map/ppermute | solution.py:20
  19.1 1.2 subtract_convert_fusion.refs_4_
  20.7 1.2 copy.16
  21.8 14.0 %all-to-all-start = ((bf16[256,2,384]{2,1,0:T(2,128)(2,1)}), bf16[256,2,384]{2,1,0:T(2,128)(2,1)S(1)}, u32[]{:S(2)}, u32[]{:S(2)}) async-start(bf16[256,2,384]{2,1,0:T(2,128)(2,1)} %copy.16), calls=%async_computation | async-start | bytes 786432 | tf_op jit(solution)/shard_map/all_to_all | solution.py:159
  41.8 12.4 %all-to-all-done = bf16[256,2,384]{2,1,0:T(2,128)(2,1)S(1)} async-done(((bf16[256,2,384]{2,1,0:T(2,128)(2,1)}), bf16[256,2,384]{2,1,0:T(2,128)(2,1)S(1)}, u32[]{:S(2)}, u32[]{:S(2)}) %all-to-all-start) | async-done | bytes 393248 | tf_op jit(solution)/shard_map/all_to_all | solution.py:159
  54.4 1.1 collective-permute-start.17
  55.6 1.0 collective-permute-start.8
  56.7 1.0 collective-permute-start.16
  57.7 1.1 collective-permute-start.15
  58.8 15.9 %collective-permute-done.17.refs_8_ = bf16[128,1536]{1,0:T(8,128)(2,1)S(1)} collective-permute-done((bf16[128,1536]{1,0:T(8,128)(2,1)S(1)}, bf16[128,1536]{1,0:T(8,128)(2,1)S(1)}, u32[]{:S(2)}, u32[]{:S(2)}) %collective-permute-start.17) | collective-permute-done | bytes 393248 | tf_op jit(solution)/shard_map/ppermute | solution.py:20
  74.8 4.3 %collective-permute-start.20 = (bf16[128,1536]{1,0:T(8,128)(2,1)S(1)}, bf16[128,1536]{1,0:T(8,128)(2,1)}, u32[]{:S(2)}, u32[]{:S(2)}) collective-permute-start(bf16[128,1536]{1,0:T(8,128)(2,1)S(1)} %collective-permute-done.17.refs_8_), channel_id=1, source_target_pairs={{0,6},{1,7},{2,0},{3,1},{4,2},{5,3},{6,4},{7,5},{8,14},{9,15},{10,... | collective-permute-start | bytes 1179656 | tf_op jit(solution)/shard_map/ppermute | solution.py:20
  79.1 4.1 %collective-permute-done.9 = bf16[2,3,8,2,384]{4,2,1,3,0:T(8,128)(2,1)S(1)} collective-permute-done((bf16[2,3,8,2,384]{4,2,1,3,0:T(8,128)(2,1)S(1)}, bf16[2,3,8,2,384]{4,2,1,3,0:T(8,128)(2,1)S(1)}, u32[]{:S(2)}, u32[]{:S(2)}) %collective-permute-start.9) | collective-permute-done | bytes 73760 | tf_op jit(solution)/shard_map/ppermute | solution.py:20
  83.2 3.4 %collective-permute-start.10 = (bf16[2,3,8,2,384]{4,2,1,3,0:T(8,128)(2,1)S(1)}, bf16[2,3,8,2,384]{4,2,1,3,0:T(8,128)(2,1)S(1)}, u32[]{:S(2)}, u32[]{:S(2)}) collective-permute-start(bf16[2,3,8,2,384]{4,2,1,3,0:T(8,128)(2,1)S(1)} %get-tuple-element.6), channel_id=1, source_target_pairs={{0,48},{8,56},{16,0},{24,8},{32,16},{40,24},{48,32},{56,40},{64,11... | collective-permute-start | bytes 221192 | tf_op jit(solution)/shard_map/ppermute | solution.py:20
  86.6 1.4 %collective-permute-done.10 = bf16[2,3,8,2,384]{4,2,1,3,0:T(8,128)(2,1)S(1)} collective-permute-done((bf16[2,3,8,2,384]{4,2,1,3,0:T(8,128)(2,1)S(1)}, bf16[2,3,8,2,384]{4,2,1,3,0:T(8,128)(2,1)S(1)}, u32[]{:S(2)}, u32[]{:S(2)}) %collective-permute-start.10) | collective-permute-done | bytes 73760 | tf_op jit(solution)/shard_map/ppermute | solution.py:20
  88.0 0.7 collective-permute-start.19
  89.3 0.8 collective-permute-start.13
  90.1 1.5 %collective-permute-start.12 = (bf16[48,3072]{1,0:T(8,128)(2,1)S(1)}, bf16[48,3072]{1,0:T(8,128)(2,1)S(1)}, u32[]{:S(2)}, u32[]{:S(2)}) collective-permute-start(bf16[48,3072]{1,0:T(8,128)(2,1)S(1)} %bitcast.50), channel_id=1, source_target_pairs={{0,128},{8,136},{16,144},{24,152},{32,160},{40,168},{48,176},{56,1... | collective-permute-start | bytes 884744 | tf_op jit(solution)/shard_map/ppermute | solution.py:20
  91.5 1.3 %fusion.1 = (s32[1,1]{1,0:T(1,128)}, s32[1,1]{1,0:T(1,128)}, s32[1,1]{1,0:T(1,128)}) fusion(s32[32,32]{1,0:T(8,128)} %param.5, s32[]{:T(128)S(6)} %select_n.32, s32[]{:T(128)S(6)} %select_n.30, s32[]{:T(128)S(6)} %select_n.29, s32[]{:T(128)S(6)} %select_n.31), kind=kLoop, calls=%fused_computation.20 | loop fusion | bytes 40 | tf_op jit(solution)/shard_map/dynamic_slice | solution.py:174
  92.9 2.4 %stack.85.index_ref = s32[15]{0:T(128)} concatenate(s32[1]{0:T(128)} %bitcast, s32[1]{0:T(128)} %bitcast.1, s32[1]{0:T(128)} %bitcast.2, s32[1]{0:T(128)} %bitcast.3, s32[1]{0:T(128)} %bitcast.4, s32[1]{0:T(128)} %bitcast.5, s32[1]{0:T(128)} %bitcast.6, s32[1]{0:T(128)} %bitcast.7, s32[1]{0:T(128)} %bitcast.8, s32[1]{0:T(128)} %bitcast.9, s32[1]{0:T(128)} %bitcast.10, ...), dimensions={0} | concatenate | bytes 120 | tf_op jit(solution)/shard_map/stack | solution.py:175
  95.3 2.3 %collective-permute-done.19.refs_10_ = bf16[128,1536]{1,0:T(8,128)(2,1)} collective-permute-done((bf16[128,1536]{1,0:T(8,128)(2,1)S(1)}, bf16[128,1536]{1,0:T(8,128)(2,1)}, u32[]{:S(2)}, u32[]{:S(2)}) %collective-permute-start.19) | collective-permute-done | bytes 393248 | tf_op jit(solution)/shard_map/ppermute | solution.py:20
  97.6 11.4 %collective-permute-done.18.refs_9_ = bf16[128,1536]{1,0:T(8,128)(2,1)S(1)} collective-permute-done((bf16[128,1536]{1,0:T(8,128)(2,1)S(1)}, bf16[128,1536]{1,0:T(8,128)(2,1)S(1)}, u32[]{:S(2)}, u32[]{:S(2)}) %collective-permute-start.18) | collective-permute-done | bytes 393248 | tf_op jit(solution)/shard_map/ppermute | solution.py:20
  109.0 0.7 copy-done.7
  109.9 0.7 copy-done.10
  110.6 20.9 %shard_map.37 = f32[3,81,16,128]{3,2,1,0:T(8,128)} custom-call(s32[15]{0:T(128)} %stack.85.index_ref, bf16[48,3072]{1,0:T(8,128)(2,1)} %bitcast.52, bf16[48,3072]{1,0:T(8,128)(2,1)} %copy-done.10, bf16[48,3072]{1,0:T(8,128)(2,1)} %copy-done.9, bf16[48,3072]{1,0:T(8,128)(2,1)} %copy-done.8, bf16[128,1536]{1,0:T(8,128)(2,1)} %copy-done, ...), custom_call_target="tpu_custom_call" | custom-call | flops 12381585408 | bytes 6291456 | tf_op jit(solution)/shard_map/pallas_call | solution.py:123
  (62 shorter events, 3.3 us)
Async XLA Ops:
  1.2 4.2 %collective-permute-start = (f32[1536]{0:T(1024)S(1)}, f32[1536]{0:T(1024)S(1)}, u32[]{:S(2)}, u32[]{:S(2)}) collective-permute-start(f32[1536]{0:T(1024)S(1)} %reduce_sum.9), channel_id=1, source_target_pairs={{0,8},{8,0},{16,24},{24,16},{32,40},{40,32},{48,56},{56,48},{64,72... | collective-permute-start | bytes 18440 | tf_op jit(solution)/shard_map/ppermute | solution.py:20
  5.3 3.4 %collective-permute-start.3 = (f32[1536]{0:T(1024)S(1)}, f32[1536]{0:T(1024)S(1)}, u32[]{:S(2)}, u32[]{:S(2)}) collective-permute-start(f32[1536]{0:T(1024)S(1)} %add.53), channel_id=1, source_target_pairs={{0,48},{8,56},{16,0},{24,8},{32,16},{40,24},{48,32},{56,40},{64,11... | collective-permute-start | bytes 18440 | tf_op jit(solution)/shard_map/ppermute | solution.py:20
  8.0 3.4 %collective-permute-start.2 = (f32[1536]{0:T(1024)S(1)}, f32[1536]{0:T(1024)S(1)}, u32[]{:S(2)}, u32[]{:S(2)}) collective-permute-start(f32[1536]{0:T(1024)S(1)} %add.53), channel_id=1, source_target_pairs={{0,32},{8,40},{16,48},{24,56},{32,0},{40,8},{48,16},{56,24},{64,96... | collective-permute-start | bytes 18440 | tf_op jit(solution)/shard_map/ppermute | solution.py:20
  8.0 4.3 %collective-permute-start.1 = (f32[1536]{0:T(1024)S(1)}, f32[1536]{0:T(1024)S(1)}, u32[]{:S(2)}, u32[]{:S(2)}) collective-permute-start(f32[1536]{0:T(1024)S(1)} %add.53), channel_id=1, source_target_pairs={{0,16},{8,24},{16,32},{24,40},{32,48},{40,56},{48,0},{56,8},{64,80... | collective-permute-start | bytes 18440 | tf_op jit(solution)/shard_map/ppermute | solution.py:20
  12.3 3.8 %collective-permute-start.6 = (f32[1536]{0:T(1024)S(1)}, f32[1536]{0:T(1024)S(1)}, u32[]{:S(2)}, u32[]{:S(2)}) collective-permute-start(f32[1536]{0:T(1024)S(1)} %add_add_fusion), channel_id=1, source_target_pairs={{0,192},{8,200},{16,208},{24,216},{32,224},{40,232},{48,240},{56,2... | collective-permute-start | bytes 18440 | tf_op jit(solution)/shard_map/ppermute | solution.py:20
  15.0 4.0 %collective-permute-start.5 = (f32[1536]{0:T(1024)S(1)}, f32[1536]{0:T(1024)S(1)}, u32[]{:S(2)}, u32[]{:S(2)}) collective-permute-start(f32[1536]{0:T(1024)S(1)} %add_add_fusion), channel_id=1, source_target_pairs={{0,128},{8,136},{16,144},{24,152},{32,160},{40,168},{48,176},{56,1... | collective-permute-start | bytes 18440 | tf_op jit(solution)/shard_map/ppermute | solution.py:20
  15.4 3.7 %collective-permute-start.4 = (f32[1536]{0:T(1024)S(1)}, f32[1536]{0:T(1024)S(1)}, u32[]{:S(2)}, u32[]{:S(2)}) collective-permute-start(f32[1536]{0:T(1024)S(1)} %add_add_fusion), channel_id=1, source_target_pairs={{0,64},{8,72},{16,80},{24,88},{32,96},{40,104},{48,112},{56,120},{... | collective-permute-start | bytes 18440 | tf_op jit(solution)/shard_map/ppermute | solution.py:20
  19.1 16.7 %copy-start.2 = (s32[3]{0:T(128)S(1)}, s32[3]{0:T(128)}, u32[]{:S(2)}) copy-start(s32[3]{0:T(128)} %param.4) | copy-start | bytes 40
  20.3 38.5 %copy-start = (bf16[128,1536]{1,0:T(8,128)(2,1)}, bf16[128,1536]{1,0:T(8,128)(2,1)S(1)}, u32[]{:S(2)}) copy-start(bf16[128,1536]{1,0:T(8,128)(2,1)S(1)} %subtract_convert_fusion.refs_4_) | copy-start | bytes 1179652
  21.8 32.4 %all-to-all-start = ((bf16[256,2,384]{2,1,0:T(2,128)(2,1)}), bf16[256,2,384]{2,1,0:T(2,128)(2,1)S(1)}, u32[]{:S(2)}, u32[]{:S(2)}) async-start(bf16[256,2,384]{2,1,0:T(2,128)(2,1)} %copy.16), calls=%async_computation | async-start | bytes 786432 | tf_op jit(solution)/shard_map/all_to_all | solution.py:159
  54.3 1.3 collective-permute-start.7
  54.4 20.3 %collective-permute-start.17 = (bf16[128,1536]{1,0:T(8,128)(2,1)S(1)}, bf16[128,1536]{1,0:T(8,128)(2,1)S(1)}, u32[]{:S(2)}, u32[]{:S(2)}) collective-permute-start(bf16[128,1536]{1,0:T(8,128)(2,1)S(1)} %subtract_convert_fusion.refs_4_), channel_id=1, source_target_pairs={{0,1},{1,0},{2,3},{3,2},{4,5},{5,4},{6,7},{7,6},{8,9},{9,8},{10,11... | collective-permute-start | bytes 1179656 | tf_op jit(solution)/shard_map/ppermute | solution.py:20
  55.6 23.5 %collective-permute-start.8 = (bf16[2,3,8,2,384]{4,2,1,3,0:T(8,128)(2,1)S(1)}, bf16[2,3,8,2,384]{4,2,1,3,0:T(8,128)(2,1)S(1)}, u32[]{:S(2)}, u32[]{:S(2)}) collective-permute-start(bf16[2,3,8,2,384]{4,2,1,3,0:T(8,128)(2,1)S(1)} %get-tuple-element.6), channel_id=1, source_target_pairs={{0,16},{8,24},{16,32},{24,40},{32,48},{40,56},{48,0},{56,8},{64,80... | collective-permute-start | bytes 221192 | tf_op jit(solution)/shard_map/ppermute | solution.py:20
  56.7 32.2 %collective-permute-start.16 = (bf16[128,1536]{1,0:T(8,128)(2,1)S(1)}, bf16[128,1536]{1,0:T(8,128)(2,1)S(1)}, u32[]{:S(2)}, u32[]{:S(2)}) collective-permute-start(bf16[128,1536]{1,0:T(8,128)(2,1)S(1)} %subtract_convert_fusion.refs_4_), channel_id=1, source_target_pairs={{0,6},{1,7},{2,0},{3,1},{4,2},{5,3},{6,4},{7,5},{8,14},{9,15},{10,... | collective-permute-start | bytes 1179656 | tf_op jit(solution)/shard_map/ppermute | solution.py:20
  57.7 31.6 %collective-permute-start.15 = (bf16[128,1536]{1,0:T(8,128)(2,1)S(1)}, bf16[128,1536]{1,0:T(8,128)(2,1)S(1)}, u32[]{:S(2)}, u32[]{:S(2)}) collective-permute-start(bf16[128,1536]{1,0:T(8,128)(2,1)S(1)} %subtract_convert_fusion.refs_4_), channel_id=1, source_target_pairs={{0,4},{1,5},{2,6},{3,7},{4,0},{5,1},{6,2},{7,3},{8,12},{9,13},{10,... | collective-permute-start | bytes 1179656 | tf_op jit(solution)/shard_map/ppermute | solution.py:20
  58.8 31.3 %collective-permute-start.14 = (bf16[128,1536]{1,0:T(8,128)(2,1)S(1)}, bf16[128,1536]{1,0:T(8,128)(2,1)S(1)}, u32[]{:S(2)}, u32[]{:S(2)}) collective-permute-start(bf16[128,1536]{1,0:T(8,128)(2,1)S(1)} %subtract_convert_fusion.refs_4_), channel_id=1, source_target_pairs={{0,2},{1,3},{2,4},{3,5},{4,6},{5,7},{6,0},{7,1},{8,10},{9,11},{10,... | collective-permute-start | bytes 1179656 | tf_op jit(solution)/shard_map/ppermute | solution.py:20
  74.7 14.5 %copy-start.3 = (bf16[128,1536]{1,0:T(8,128)(2,1)}, bf16[128,1536]{1,0:T(8,128)(2,1)S(1)}, u32[]{:S(2)}) copy-start(bf16[128,1536]{1,0:T(8,128)(2,1)S(1)} %collective-permute-done.17.refs_8_) | copy-start | bytes 1179652
  74.8 16.8 %collective-permute-start.20 = (bf16[128,1536]{1,0:T(8,128)(2,1)S(1)}, bf16[128,1536]{1,0:T(8,128)(2,1)}, u32[]{:S(2)}, u32[]{:S(2)}) collective-permute-start(bf16[128,1536]{1,0:T(8,128)(2,1)S(1)} %collective-permute-done.17.refs_8_), channel_id=1, source_target_pairs={{0,6},{1,7},{2,0},{3,1},{4,2},{5,3},{6,4},{7,5},{8,14},{9,15},{10,... | collective-permute-start | bytes 1179656 | tf_op jit(solution)/shard_map/ppermute | solution.py:20
  79.1 4.1 %collective-permute-start.9 = (bf16[2,3,8,2,384]{4,2,1,3,0:T(8,128)(2,1)S(1)}, bf16[2,3,8,2,384]{4,2,1,3,0:T(8,128)(2,1)S(1)}, u32[]{:S(2)}, u32[]{:S(2)}) collective-permute-start(bf16[2,3,8,2,384]{4,2,1,3,0:T(8,128)(2,1)S(1)} %get-tuple-element.6), channel_id=1, source_target_pairs={{0,32},{8,40},{16,48},{24,56},{32,0},{40,8},{48,16},{56,24},{64,96... | collective-permute-start | bytes 221192 | tf_op jit(solution)/shard_map/ppermute | solution.py:20
  83.2 4.8 %collective-permute-start.10 = (bf16[2,3,8,2,384]{4,2,1,3,0:T(8,128)(2,1)S(1)}, bf16[2,3,8,2,384]{4,2,1,3,0:T(8,128)(2,1)S(1)}, u32[]{:S(2)}, u32[]{:S(2)}) collective-permute-start(bf16[2,3,8,2,384]{4,2,1,3,0:T(8,128)(2,1)S(1)} %get-tuple-element.6), channel_id=1, source_target_pairs={{0,48},{8,56},{16,0},{24,8},{32,16},{40,24},{48,32},{56,40},{64,11... | collective-permute-start | bytes 221192 | tf_op jit(solution)/shard_map/ppermute | solution.py:20
  88.0 9.6 %collective-permute-start.19 = (bf16[128,1536]{1,0:T(8,128)(2,1)S(1)}, bf16[128,1536]{1,0:T(8,128)(2,1)}, u32[]{:S(2)}, u32[]{:S(2)}) collective-permute-start(bf16[128,1536]{1,0:T(8,128)(2,1)S(1)} %collective-permute-done.17.refs_8_), channel_id=1, source_target_pairs={{0,4},{1,5},{2,6},{3,7},{4,0},{5,1},{6,2},{7,3},{8,12},{9,13},{10,... | collective-permute-start | bytes 1179656 | tf_op jit(solution)/shard_map/ppermute | solution.py:20
  88.9 20.1 %copy-start.4 = (bf16[128,1536]{1,0:T(8,128)(2,1)}, bf16[128,1536]{1,0:T(8,128)(2,1)S(1)}, u32[]{:S(2)}) copy-start(bf16[128,1536]{1,0:T(8,128)(2,1)S(1)} %collective-permute-done.16.refs_7_) | copy-start | bytes 1179652
  88.9 20.0 %collective-permute-start.18 = (bf16[128,1536]{1,0:T(8,128)(2,1)S(1)}, bf16[128,1536]{1,0:T(8,128)(2,1)S(1)}, u32[]{:S(2)}, u32[]{:S(2)}) collective-permute-start(bf16[128,1536]{1,0:T(8,128)(2,1)S(1)} %collective-permute-done.17.refs_8_), channel_id=1, source_target_pairs={{0,2},{1,3},{2,4},{3,5},{4,6},{5,7},{6,0},{7,1},{8,10},{9,11},{10,... | collective-permute-start | bytes 1179656 | tf_op jit(solution)/shard_map/ppermute | solution.py:20
  89.3 19.8 %copy-start.1 = (bf16[6,8,8,384]{3,1,2,0:T(8,128)(2,1)}, bf16[6,8,8,384]{3,1,2,0:T(8,128)(2,1)S(1)}, u32[]{:S(2)}) copy-start(bf16[6,8,8,384]{3,1,2,0:T(8,128)(2,1)S(1)} %copy.21) | copy-start | bytes 884740
  89.3 19.7 %copy-start.5 = (bf16[128,1536]{1,0:T(8,128)(2,1)}, bf16[128,1536]{1,0:T(8,128)(2,1)S(1)}, u32[]{:S(2)}) copy-start(bf16[128,1536]{1,0:T(8,128)(2,1)S(1)} %collective-permute-done.15.refs_6_) | copy-start | bytes 1179652
  89.3 19.7 %collective-permute-start.13 = (bf16[48,3072]{1,0:T(8,128)(2,1)S(1)}, bf16[48,3072]{1,0:T(8,128)(2,1)S(1)}, u32[]{:S(2)}, u32[]{:S(2)}) collective-permute-start(bf16[48,3072]{1,0:T(8,128)(2,1)S(1)} %bitcast.49), channel_id=1, source_target_pairs={{0,192},{8,200},{16,208},{24,216},{32,224},{40,232},{48,240},{56,2... | collective-permute-start | bytes 884744 | tf_op jit(solution)/shard_map/ppermute | solution.py:20
  90.1 19.0 %copy-start.6 = (bf16[128,1536]{1,0:T(8,128)(2,1)}, bf16[128,1536]{1,0:T(8,128)(2,1)S(1)}, u32[]{:S(2)}) copy-start(bf16[128,1536]{1,0:T(8,128)(2,1)S(1)} %collective-permute-done.14.refs_5_) | copy-start | bytes 1179652
  90.1 18.9 %collective-permute-start.12 = (bf16[48,3072]{1,0:T(8,128)(2,1)S(1)}, bf16[48,3072]{1,0:T(8,128)(2,1)S(1)}, u32[]{:S(2)}, u32[]{:S(2)}) collective-permute-start(bf16[48,3072]{1,0:T(8,128)(2,1)S(1)} %bitcast.50), channel_id=1, source_target_pairs={{0,128},{8,136},{16,144},{24,152},{32,160},{40,168},{48,176},{56,1... | collective-permute-start | bytes 884744 | tf_op jit(solution)/shard_map/ppermute | solution.py:20
  91.5 17.4 %collective-permute-start.11 = (bf16[48,3072]{1,0:T(8,128)(2,1)S(1)}, bf16[48,3072]{1,0:T(8,128)(2,1)S(1)}, u32[]{:S(2)}, u32[]{:S(2)}) collective-permute-start(bf16[48,3072]{1,0:T(8,128)(2,1)S(1)} %bitcast.51), channel_id=1, source_target_pairs={{0,64},{8,72},{16,80},{24,88},{32,96},{40,104},{48,112},{56,120},{... | collective-permute-start | bytes 884744 | tf_op jit(solution)/shard_map/ppermute | solution.py:20
  109.0 0.7 copy-start.7
  109.0 0.8 copy-start.8
  109.0 0.9 copy-start.9
  (1 other events, 0.7 us)

commit v2 on v1

v2 whole, which is shorter than its diff:
```python
import functools
import math

import jax
import jax.numpy as jnp
from jax import lax
from jax.experimental import pallas as pl
from jax.experimental.pallas import tpu as pltpu
from jax.sharding import PartitionSpec as P

LAG = 40
STEPS = 3
LAGS = 2 * LAG + 1
HALF = LAG + 1
EDGE = 128


def permute(value, axis, target):
    size = lax.axis_size(axis)
    return lax.ppermute(value, axis, [(i, target(i)) for i in range(size)])


def core_flip(i):
    return i ^ 1


def z_shift(d):
    return lambda i: (i & ~6) | ((((i >> 1) + d) & 3) << 1)


def y_shift(d):
    return lambda i: (i & 7) | ((((i >> 3) + d) & 3) << 3)


def hi_flip(i):
    return i ^ 1


def x_shift(d):
    return lambda i: (i & 1) | ((((i >> 1) + d) & 3) << 1)


def z_flip(bit):
    return lambda i: i ^ (2 << bit)


def join(mine, other, bit):
    return jnp.where(bit == 0, jnp.stack([mine, other]), jnp.stack([other, mine]))


def around_z(value, here):
    for bit in range(2):
        value = join(value, permute(value, "chan", z_flip(bit)), (here >> bit) & 1)
    return value.reshape((4,) + value.shape[2:])


def around_y(value, here):
    after, before = permute(value, "chan", y_shift(1)), permute(value, "chan", y_shift(3))
    value, after, before = lax.optimization_barrier((value, after, before))
    ring = [value, after, permute(value, "chan", y_shift(2)), before]
    ring = jnp.stack(ring[::-1] + ring[::-1])
    return lax.dynamic_slice_in_dim(ring, 3 - here, 4, 0)


def correlate_kernel(place_ref, owners_ref, mask_ref, *refs, span, chunk):
    own_refs, block_refs = refs[:2], refs[2:10]
    out_ref, own, block, left, right, total = refs[10:]
    chan, win = place_ref[0], place_ref[1]
    core, x, hi = chan & 1, win >> 1, win & 1
    rows = own.shape[0]
    share = rows // STEPS
    width = block.shape[0]
    length = block.shape[1] - EDGE
    quarter = span // 4
    bf16 = jnp.bfloat16

    own[:, :EDGE] = jnp.zeros((rows, EDGE), bf16)
    own[:, EDGE + length:] = jnp.zeros((rows, EDGE), bf16)
    block[:, length:] = jnp.zeros((width, EDGE), bf16)
    own_power = jnp.zeros((rows, EDGE), jnp.float32)
    slices = length // span
    for k in range(4 * slices):
        d, half, w = k // (2 * slices), k // slices % 2, k % slices
        where = 2 * half + (core ^ d)
        at = (half * slices + w) * quarter
        piece = own_refs[d][:, at:at + quarter]
        start = pl.multiple_of(EDGE + w * span + where * quarter, EDGE)
        own[:, pl.ds(start, quarter)] = piece
        wide = piece.astype(jnp.float32)
        for k in range(quarter // EDGE):
            part = wide[:, k * EDGE:(k + 1) * EDGE]
            own_power += part * part
    block_power = jnp.zeros((width, EDGE), jnp.float32)
    for d in range(8):
        piece = block_refs[d][...]
        slot = (((x - d) & 3) << 1) | (hi if d < 4 else 1 - hi)
        start = pl.multiple_of(slot * span, EDGE)
        block[:, pl.ds(start, span)] = piece
        wide = piece.astype(jnp.float32)
        for k in range(span // EDGE):
            part = wide[:, k * EDGE:(k + 1) * EDGE]
            block_power += part * part
    own_power = jnp.sum(own_power, axis=1, keepdims=True) / length
    block_power = jnp.sum(block_power, axis=1, keepdims=True) / length
    own_scale = 1.0 / jnp.sqrt(own_power + 1e-06)
    block_scale = 1.0 / jnp.sqrt(block_power + 1e-06)
    block_scale = jnp.transpose(jnp.broadcast_to(block_scale, (width, width)))[:1]

    def product(a, b):
        return lax.dot_general(a, b, (((1,), (1,)), ((), ())), preferred_element_type=jnp.float32)

    lead = own[:, :2 * EDGE]
    before = jnp.concatenate([jnp.zeros((width, EDGE - HALF), bf16), block[:, :HALF]], axis=1)
    part = HALF * share
    flags = [mask_ref[owners_ref[s], chan] for s in range(STEPS)]
    for k in range(0, length, chunk):
        right[:width] = block[:, k:k + chunk]
        right[width:] = block[:, HALF + k:HALF + k + chunk]
        for s in range(STEPS):
            @pl.when(flags[s] != 0)
            def _():
                if k == 0:
                    for l in range(HALF):
                        left[l * share:(l + 1) * share, :EDGE] = lead[s * share:(s + 1) * share, LAG - l:LAG - l + EDGE]
                    at = slice(s * part, (s + 1) * part)
                    total[at, :width] = jnp.zeros((part, width), jnp.float32)
                    total[at, width:] = product(left[:, :EDGE], before)
                mine = own[s * share:(s + 1) * share, k + EDGE:k + chunk + 2 * EDGE]
                for g in range(0, HALF, 21):
                    stop = min(g + 21, HALF)
                    for l in range(g, stop):
                        left[l * share:(l + 1) * share] = mine[:, LAG - l:LAG - l + chunk]
                    at = slice(s * part + g * share, s * part + stop * share)
                    total[at] += product(left[g * share:stop * share], right[...])

    norm = 1.0 / math.sqrt(length)
    for s in range(STEPS):
        scale = own_scale[s * share:(s + 1) * share] * (block_scale * norm)

        @pl.when(flags[s] != 0)
        def _():
            wide = scale * flags[s].astype(jnp.float32)
            for l in range(HALF):
                at = slice(s * part + l * share, s * part + (l + 1) * share)
                out_ref[s, l] = total[at, :width] * wide
                if l + HALF < LAGS:
                    out_ref[s, l + HALF] = total[at, width:] * wide

        @pl.when(flags[s] == 0)
        def _():
            out_ref[s] = jnp.zeros((LAGS, share, width), jnp.float32)


def correlate(place, owners, pair_mask, own, block):
    rows, width, span = own[0].shape[0], block[0].shape[0], block[0].shape[1]
    length = span * len(block)
    chunk = 12288
    vmem = pl.BlockSpec(memory_space=pltpu.VMEM)
    return pl.pallas_call(
        functools.partial(correlate_kernel, span=span, chunk=chunk),
        out_shape=jax.ShapeDtypeStruct((STEPS, LAGS, rows // STEPS, width), jnp.float32),
        in_specs=[pl.BlockSpec(memory_space=pltpu.SMEM)] * 3 + [vmem] * 10,
        out_specs=vmem,
        scratch_shapes=[
            pltpu.VMEM((rows, length + 2 * EDGE), jnp.bfloat16),
            pltpu.VMEM((width, length + EDGE), jnp.bfloat16),
            pltpu.VMEM((HALF * rows // STEPS, chunk), jnp.bfloat16),
            pltpu.VMEM((2 * width, chunk), jnp.bfloat16),
            pltpu.VMEM((HALF * rows, 2 * width), jnp.float32),
        ],
        compiler_params=pltpu.CompilerParams(vmem_limit_bytes=56 * 2**20),
        cost_estimate=pl.CostEstimate(
            flops=2 * HALF * rows * 2 * width * length, bytes_accessed=6 * 2**20, transcendentals=0
        ),
    )(place, owners, pair_mask, *own, *block)


def local(record, owners, pair_mask):
    width, span = record.shape
    channels = width * lax.axis_size("chan")
    chan, win = lax.axis_index("chan"), lax.axis_index("win")

    sums = jnp.sum(record, axis=0)
    sums = sums + permute(sums, "chan", core_flip)
    sums = sums + (permute(sums, "chan", z_shift(1)) + permute(sums, "chan", z_shift(2)) + permute(sums, "chan", z_shift(3)))
    sums = sums + (permute(sums, "chan", y_shift(1)) + permute(sums, "chan", y_shift(2)) + permute(sums, "chan", y_shift(3)))
    cleaned = (record - (sums / channels)[None, :]).astype(jnp.bfloat16)

    far = permute(cleaned, "win", hi_flip)
    block = [cleaned] + [permute(cleaned, "win", x_shift(d)) for d in (1, 2, 3)]

    quarter = span // 4
    here = chan >= 0

    def take(value):
        pieces = value.reshape(8, 4, 2, 2, 2, 2, quarter).transpose(4, 2, 1, 5, 0, 3, 6).reshape(256, 2, quarter)
        pieces = lax.all_to_all(pieces, ("chan", "win"), 0, 0).reshape(32, 8, 2, quarter)
        chosen = owners[:, None] == jnp.arange(32, dtype=owners.dtype)
        pieces = jnp.where(chosen[:, :, None, None, None], pieces, jnp.zeros_like(pieces)).astype(jnp.float32)
        return jnp.sum(pieces, axis=1).astype(jnp.bfloat16)

    mine = lax.cond(here, take, lambda value: jnp.zeros((STEPS, 8, 2, quarter), jnp.bfloat16), cleaned)
    place = jnp.stack([chan, win])
    mine, place, far, *block = lax.optimization_barrier((mine, place, far, *block))
    block += [far] + [permute(far, "win", x_shift(d)) for d in (1, 2, 3)]

    def share(value):
        value = around_z(value, (chan >> 1) & 3)
        value = around_y(value, chan >> 3).reshape(2, 2, 4, STEPS, 8, 2, quarter)
        value = value.transpose(3, 2, 1, 5, 0, 4, 6).reshape(16 * STEPS, 2 * 8 * quarter)
        return value, permute(value, "chan", core_flip)

    def none(value):
        blank = jnp.zeros((16 * STEPS, 2 * 8 * quarter), jnp.bfloat16)
        return blank, blank

    own = lax.cond(here, share, none, mine)
    own, *block = lax.optimization_barrier((own, *block))
    return correlate(place, owners, pair_mask, own, block)


def solution(mesh):
    in_specs = (P("chan", "win"), P(), P())
    out_specs = P(None, None, "win", "chan")
    return jax.shard_map(local, mesh=mesh, in_specs=in_specs, out_specs=out_specs, check_vma=False)
```

time: 132 us -> 106 us (0.80)
  the two profiles are of different devices: /device:TPU:1 before, /device:TPU:19 now
where the time goes in v2:
time: 106 us; the launch traced here: 105 us
  starting transfers between devices  43.7 us (41%)
  waiting for transfers between devices  39.2 us (37%)
  Pallas kernels  15.5 us (15%)
  local copies, waits for them, and re-layouts  4.01 us (4%)
  other arithmetic  2.34 us (2%)
    ppermute x20, starting transfers between devices, permute(): return lax.ppermute(value, axis, [(i, target(i)) for i in range(size)])  32 us
    ppermute x20, waiting for transfers between devices, permute(): return lax.ppermute(value, axis, [(i, target(i)) for i in range(size)])  24 us
    pallas_call x1, Pallas kernels, correlate(): pl.pallas_call(functools.partial(correlate_kernel, span=span, chunk=chunk...  15.5 us
    all_to_all x1, waiting for transfers between devices, take(): lax.all_to_all(pieces, ('chan', 'win'), 0, 0).reshape(32, 8, 2, quarter)  15.1 us
    all_to_all x1, starting transfers between devices, take(): lax.all_to_all(pieces, ('chan', 'win'), 0, 0).reshape(32, 8, 2, quarter)  11.7 us
  transfers between devices with their start and end apart: 21, of which 13 were waited for; matrix products, arithmetic and copies ran while one was open for 4% of the time, Pallas kernels for 0%

profile of v2, /device:TPU:19, one launch (start us, length us, event | category | flops | bytes accessed | tf_op | source)
XLA Modules:
  0.0 104.9 jit_solution(8785126914540359723)
XLA Ops:
  0.0 1.3 %reduce_sum.21 = f32[1536]{0:T(1024)S(1)} reduce(f32[128,1536]{1,0:T(8,128)} %param.7, f32[]{:T(128)} %constant.30.clone.1), dimensions={0}, to_apply=%region_0.0 | reduce | flops 195072 | bytes 792580 | tf_op jit(solution)/shard_map/reduce_sum | solution.py:183
  1.3 0.8 collective-permute-start.6
  2.0 0.8 collective-permute-done.6
  2.9 4.3 %collective-permute-start.9 = (f32[1536]{0:T(1024)S(1)}, f32[1536]{0:T(1024)S(1)}, u32[]{:S(2)}, u32[]{:S(2)}) collective-permute-start(f32[1536]{0:T(1024)S(1)} %add.25), channel_id=1, source_target_pairs={{0,48},{8,56},{16,0},{24,8},{32,16},{40,24},{48,32},{56,40},{64,11... | collective-permute-start | bytes 18440 | tf_op jit(solution)/shard_map/ppermute | solution.py:20
  8.0 2.6 %collective-permute-done.8 = f32[1536]{0:T(1024)S(1)} collective-permute-done((f32[1536]{0:T(1024)S(1)}, f32[1536]{0:T(1024)S(1)}, u32[]{:S(2)}, u32[]{:S(2)}) %collective-permute-start.8) | collective-permute-done | bytes 6176 | tf_op jit(solution)/shard_map/ppermute | solution.py:20
  10.6 0.9 collective-permute-done.7
  11.7 2.6 %collective-permute-start.11 = (f32[1536]{0:T(1024)S(1)}, f32[1536]{0:T(1024)S(1)}, u32[]{:S(2)}, u32[]{:S(2)}) collective-permute-start(f32[1536]{0:T(1024)S(1)} %add_add_fusion), channel_id=1, source_target_pairs={{0,128},{8,136},{16,144},{24,152},{32,160},{40,168},{48,176},{56,1... | collective-permute-start | bytes 18440 | tf_op jit(solution)/shard_map/ppermute | solution.py:20
  14.3 1.4 %collective-permute-done.11 = f32[1536]{0:T(1024)S(1)} collective-permute-done((f32[1536]{0:T(1024)S(1)}, f32[1536]{0:T(1024)S(1)}, u32[]{:S(2)}, u32[]{:S(2)}) %collective-permute-start.11) | collective-permute-done | bytes 6176 | tf_op jit(solution)/shard_map/ppermute | solution.py:20
  15.7 1.1 %collective-permute-done.10 = f32[1536]{0:T(1024)S(1)} collective-permute-done((f32[1536]{0:T(1024)S(1)}, f32[1536]{0:T(1024)S(1)}, u32[]{:S(2)}, u32[]{:S(2)}) %collective-permute-start.10) | collective-permute-done | bytes 6176 | tf_op jit(solution)/shard_map/ppermute | solution.py:20
  17.2 2.1 %collective-permute-start.15 = (bf16[128,1536]{1,0:T(8,128)(2,1)S(1)}, bf16[128,1536]{1,0:T(8,128)(2,1)S(1)}, u32[]{:S(2)}, u32[]{:S(2)}) collective-permute-start(bf16[128,1536]{1,0:T(8,128)(2,1)S(1)} %subtract_convert_fusion.refs_2_), channel_id=1, source_target_pairs={{0,4},{1,5},{2,6},{3,7},{4,0},{5,1},{6,2},{7,3},{8,12},{9,13},{10,... | collective-permute-start | bytes 1179656 | tf_op jit(solution)/shard_map/ppermute | solution.py:20
  19.3 1.5 %collective-permute-start.14 = (bf16[128,1536]{1,0:T(8,128)(2,1)S(1)}, bf16[128,1536]{1,0:T(8,128)(2,1)S(1)}, u32[]{:S(2)}, u32[]{:S(2)}) collective-permute-start(bf16[128,1536]{1,0:T(8,128)(2,1)S(1)} %subtract_convert_fusion.refs_2_), channel_id=1, source_target_pairs={{0,2},{1,3},{2,4},{3,5},{4,6},{5,7},{6,0},{7,1},{8,10},{9,11},{10,... | collective-permute-start | bytes 1179656 | tf_op jit(solution)/shard_map/ppermute | solution.py:20
  20.9 4.5 %collective-permute-start.13 = (bf16[128,1536]{1,0:T(8,128)(2,1)S(1)}, bf16[128,1536]{1,0:T(8,128)(2,1)S(1)}, u32[]{:S(2)}, u32[]{:S(2)}) collective-permute-start(bf16[128,1536]{1,0:T(8,128)(2,1)S(1)} %subtract_convert_fusion.refs_2_), channel_id=1, source_target_pairs={{0,1},{1,0},{2,3},{3,2},{4,5},{5,4},{6,7},{7,6},{8,9},{9,8},{10,11... | collective-permute-start | bytes 1179656 | tf_op jit(solution)/shard_map/ppermute | solution.py:20
  25.4 0.7 pad_add_fusion.place_ref
  26.0 28.8 %conditional.2 = (bf16[3,8,2,384]{3,1,2,0:T(8,128)(2,1)S(1)}) conditional(s32[]{:T(128)} %convert_element_type.6, () %tuple.22, (s32[3]{0:T(128)S(1)}, bf16[128,1536]{1,0:T(8,128)(2,1)S(1)}) %tuple.35), branch_computations={%region_1.0_spmd, %region_2.4_spmd} | conditional | flops 1161312 | bytes 4755700 | solution.py:202
  26.5 1.2 %copy.15 = bf16[256,2,384]{2,1,0:T(2,128)(2,1)} copy(bf16[256,2,384]{2,0,1:T(8,128)(2,1)S(1)} %bitcast.30) | data formatting | bytes 786432 | tf_op jit(solution)/shard_map/cond/branch_1_fun/reshape | solution.py:196
  27.7 11.7 %all-to-all-start = ((bf16[256,2,384]{2,1,0:T(2,128)(2,1)}), bf16[256,2,384]{2,1,0:T(2,128)(2,1)S(1)}, u32[]{:S(2)}, u32[]{:S(2)}) async-start(bf16[256,2,384]{2,1,0:T(2,128)(2,1)} %copy.15), calls=%async_computation | async-start | bytes 786432 | tf_op jit(solution)/shard_map/cond/branch_1_fun/all_to_all | solution.py:197
  39.4 15.1 %all-to-all-done = bf16[256,2,384]{2,1,0:T(2,128)(2,1)S(1)} async-done(((bf16[256,2,384]{2,1,0:T(2,128)(2,1)}), bf16[256,2,384]{2,1,0:T(2,128)(2,1)S(1)}, u32[]{:S(2)}, u32[]{:S(2)}) %all-to-all-start) | async-done | bytes 393248 | tf_op jit(solution)/shard_map/cond/branch_1_fun/all_to_all | solution.py:197
  54.9 1.6 %collective-permute-start.19 = (bf16[128,1536]{1,0:T(8,128)(2,1)S(1)}, bf16[128,1536]{1,0:T(8,128)(2,1)S(1)}, u32[]{:S(2)}, u32[]{:S(2)}) collective-permute-start(bf16[128,1536]{1,0:T(8,128)(2,1)S(1)} %collective-permute-done.13.refs_6_), channel_id=1, source_target_pairs={{0,6},{1,7},{2,0},{3,1},{4,2},{5,3},{6,4},{7,5},{8,14},{9,15},{10,... | collective-permute-start | bytes 1179656 | tf_op jit(solution)/shard_map/ppermute | solution.py:20
  56.9 2.0 %collective-permute-start.17 = (bf16[128,1536]{1,0:T(8,128)(2,1)S(1)}, bf16[128,1536]{1,0:T(8,128)(2,1)}, u32[]{:S(2)}, u32[]{:S(2)}) collective-permute-start(bf16[128,1536]{1,0:T(8,128)(2,1)S(1)} %collective-permute-done.13.refs_6_), channel_id=1, source_target_pairs={{0,2},{1,3},{2,4},{3,5},{4,6},{5,7},{6,0},{7,1},{8,10},{9,11},{10,... | collective-permute-start | bytes 1179656 | tf_op jit(solution)/shard_map/ppermute | solution.py:20
  58.9 29.7 %conditional.3 = (bf16[48,6144]{1,0:T(8,128)(2,1)}, bf16[48,6144]{1,0:T(8,128)(2,1)}) conditional(s32[]{:T(128)} %convert_element_type.6, () %tuple.25, (s32[]{:T(128)}, bf16[3,8,2,384]{3,1,2,0:T(8,128)(2,1)S(1)}) %tuple.26), branch_computations={%region_4.5_spmd, %region_5.6_spmd} | conditional | flops 442381 | bytes 11059611 | solution.py:217
  59.0 3.1 %collective-permute-done = bf16[3,8,2,384]{3,1,2,0:T(8,128)(2,1)S(1)} collective-permute-done((bf16[3,8,2,384]{3,1,2,0:T(8,128)(2,1)S(1)}, bf16[3,8,2,384]{3,1,2,0:T(8,128)(2,1)S(1)}, u32[]{:S(2)}, u32[]{:S(2)}) %collective-permute-start) | collective-permute-done | bytes 36896 | tf_op jit(solution)/shard_map/cond/branch_1_fun/ppermute | solution.py:20
  62.2 4.6 %collective-permute-done.1 = bf16[2,3,8,2,384]{4,2,3,1,0:T(8,128)(2,1)S(1)} collective-permute-done((bf16[2,3,8,2,384]{4,2,3,1,0:T(8,128)(2,1)S(1)}, bf16[2,3,8,2,384]{4,2,3,1,0:T(8,128)(2,1)S(1)}, u32[]{:S(2)}, u32[]{:S(2)}) %collective-permute-start.1) | collective-permute-done | bytes 73760 | tf_op jit(solution)/shard_map/cond/branch_1_fun/ppermute | solution.py:20
  66.8 1.0 collective-permute-start.3
  68.4 2.9 %collective-permute-done.3 = bf16[4,3,8,2,384]{4,2,3,1,0:T(8,128)(2,1)S(1)} collective-permute-done((bf16[4,3,8,2,384]{4,2,3,1,0:T(8,128)(2,1)S(1)}, bf16[4,3,8,2,384]{4,2,3,1,0:T(8,128)(2,1)S(1)}, u32[]{:S(2)}, u32[]{:S(2)}) %collective-permute-start.3) | collective-permute-done | bytes 147488 | tf_op jit(solution)/shard_map/cond/branch_1_fun/ppermute | solution.py:20
  71.3 0.9 collective-permute-done.2
  72.2 2.7 %collective-permute-start.4 = (bf16[4,3,8,2,384]{4,2,3,1,0:T(8,128)(2,1)S(1)}, bf16[4,3,8,2,384]{4,2,3,1,0:T(8,128)(2,1)S(1)}, u32[]{:S(2)}, u32[]{:S(2)}) collective-permute-start(bf16[4,3,8,2,384]{4,2,3,1,0:T(8,128)(2,1)S(1)} %bitcast.34), channel_id=1, source_target_pairs={{0,128},{8,136},{16,144},{24,152},{32,160},{40,168},{48,176},{56,1... | collective-permute-start | bytes 442376 | tf_op jit(solution)/shard_map/cond/branch_1_fun/ppermute | solution.py:20
  74.9 3.2 %collective-permute-done.4 = bf16[4,3,8,2,384]{4,2,3,1,0:T(8,128)(2,1)S(1)} collective-permute-done((bf16[4,3,8,2,384]{4,2,3,1,0:T(8,128)(2,1)S(1)}, bf16[4,3,8,2,384]{4,2,3,1,0:T(8,128)(2,1)S(1)}, u32[]{:S(2)}, u32[]{:S(2)}) %collective-permute-start.4) | collective-permute-done | bytes 147488 | tf_op jit(solution)/shard_map/cond/branch_1_fun/ppermute | solution.py:20
  78.5 1.1 %reshape.100 = bf16[48,6144]{1,0:T(8,128)(2,1)} reshape(bf16[3,4,2,2,2,8,384]{6,5,4,3,2,1,0:T(8,128)(2,1)S(1)} %copy.17) | data formatting | bytes 1179648 | tf_op jit(solution)/shard_map/cond/branch_1_fun/reshape | solution.py:210
  79.7 6.9 %collective-permute-start.5 = (bf16[48,6144]{1,0:T(8,128)(2,1)}, bf16[48,6144]{1,0:T(8,128)(2,1)}, u32[]{:S(2)}, u32[]{:S(2)}) collective-permute-start(bf16[48,6144]{1,0:T(8,128)(2,1)} %reshape.100), channel_id=1, source_target_pairs={{0,8},{8,0},{16,24},{24,16},{32,40},{40,32},{48,56},{56,48},{64,72... | collective-permute-start | bytes 1769480 | tf_op jit(solution)/shard_map/cond/branch_1_fun/ppermute | solution.py:20
  86.6 2.0 %collective-permute-done.5 = bf16[48,6144]{1,0:T(8,128)(2,1)} collective-permute-done((bf16[48,6144]{1,0:T(8,128)(2,1)}, bf16[48,6144]{1,0:T(8,128)(2,1)}, u32[]{:S(2)}, u32[]{:S(2)}) %collective-permute-start.5) | collective-permute-done | bytes 589856 | tf_op jit(solution)/shard_map/cond/branch_1_fun/ppermute | solution.py:20
  88.6 0.7 copy-done.5
  89.5 15.5 %shard_map.37 = f32[3,81,16,128]{3,2,1,0:T(8,128)} custom-call(s32[2]{0:T(128)} %pad_add_fusion.place_ref, s32[3]{0:T(128)S(1)} %copy-done.7, s32[32,32]{1,0:T(8,128)} %mask_ref.1, bf16[48,6144]{1,0:T(8,128)(2,1)} %get-tuple-element.51.refs_0_, bf16[48,6144]{1,0:T(8,128)(2,1)} %get-tuple-element.52.refs_1_, ...), custom_call_target="tpu_custom_call" | custom-call | flops 12381585408 | bytes 6291456 | tf_op jit(solution)/shard_map/pallas_call | solution.py:159
  (55 shorter events, 3.9 us)
Async XLA Ops:
  0.0 16.8 %copy-start = (f32[128,1536]{1,0:T(8,128)S(1)}, f32[128,1536]{1,0:T(8,128)}, u32[]{:S(2)}) copy-start(f32[128,1536]{1,0:T(8,128)} %param.7) | copy-start | bytes 2359300
  0.0 26.0 %copy-start.7 = (s32[3]{0:T(128)S(1)}, s32[3]{0:T(128)}, u32[]{:S(2)}) copy-start(s32[3]{0:T(128)} %owners_ref.1) | copy-start | bytes 40
  1.3 1.6 %collective-permute-start.6 = (f32[1536]{0:T(1024)S(1)}, f32[1536]{0:T(1024)S(1)}, u32[]{:S(2)}, u32[]{:S(2)}) collective-permute-start(f32[1536]{0:T(1024)S(1)} %reduce_sum.21), channel_id=1, source_target_pairs={{0,8},{8,0},{16,24},{24,16},{32,40},{40,32},{48,56},{56,48},{64,72... | collective-permute-start | bytes 18440 | tf_op jit(solution)/shard_map/ppermute | solution.py:20
  2.9 5.1 %collective-permute-start.9 = (f32[1536]{0:T(1024)S(1)}, f32[1536]{0:T(1024)S(1)}, u32[]{:S(2)}, u32[]{:S(2)}) collective-permute-start(f32[1536]{0:T(1024)S(1)} %add.25), channel_id=1, source_target_pairs={{0,48},{8,56},{16,0},{24,8},{32,16},{40,24},{48,32},{56,40},{64,11... | collective-permute-start | bytes 18440 | tf_op jit(solution)/shard_map/ppermute | solution.py:20
  7.2 3.4 %collective-permute-start.8 = (f32[1536]{0:T(1024)S(1)}, f32[1536]{0:T(1024)S(1)}, u32[]{:S(2)}, u32[]{:S(2)}) collective-permute-start(f32[1536]{0:T(1024)S(1)} %add.25), channel_id=1, source_target_pairs={{0,32},{8,40},{16,48},{24,56},{32,0},{40,8},{48,16},{56,24},{64,96... | collective-permute-start | bytes 18440 | tf_op jit(solution)/shard_map/ppermute | solution.py:20
  7.2 4.3 %collective-permute-start.7 = (f32[1536]{0:T(1024)S(1)}, f32[1536]{0:T(1024)S(1)}, u32[]{:S(2)}, u32[]{:S(2)}) collective-permute-start(f32[1536]{0:T(1024)S(1)} %add.25), channel_id=1, source_target_pairs={{0,16},{8,24},{16,32},{24,40},{32,48},{40,56},{48,0},{56,8},{64,80... | collective-permute-start | bytes 18440 | tf_op jit(solution)/shard_map/ppermute | solution.py:20
  11.5 2.8 %collective-permute-start.12 = (f32[1536]{0:T(1024)S(1)}, f32[1536]{0:T(1024)S(1)}, u32[]{:S(2)}, u32[]{:S(2)}) collective-permute-start(f32[1536]{0:T(1024)S(1)} %add_add_fusion), channel_id=1, source_target_pairs={{0,192},{8,200},{16,208},{24,216},{32,224},{40,232},{48,240},{56,2... | collective-permute-start | bytes 18440 | tf_op jit(solution)/shard_map/ppermute | solution.py:20
  11.7 4.0 %collective-permute-start.11 = (f32[1536]{0:T(1024)S(1)}, f32[1536]{0:T(1024)S(1)}, u32[]{:S(2)}, u32[]{:S(2)}) collective-permute-start(f32[1536]{0:T(1024)S(1)} %add_add_fusion), channel_id=1, source_target_pairs={{0,128},{8,136},{16,144},{24,152},{32,160},{40,168},{48,176},{56,1... | collective-permute-start | bytes 18440 | tf_op jit(solution)/shard_map/ppermute | solution.py:20
  14.3 2.5 %collective-permute-start.10 = (f32[1536]{0:T(1024)S(1)}, f32[1536]{0:T(1024)S(1)}, u32[]{:S(2)}, u32[]{:S(2)}) collective-permute-start(f32[1536]{0:T(1024)S(1)} %add_add_fusion), channel_id=1, source_target_pairs={{0,64},{8,72},{16,80},{24,88},{32,96},{40,104},{48,112},{56,120},{... | collective-permute-start | bytes 18440 | tf_op jit(solution)/shard_map/ppermute | solution.py:20
  16.9 38.0 %collective-permute-start.16 = (bf16[128,1536]{1,0:T(8,128)(2,1)S(1)}, bf16[128,1536]{1,0:T(8,128)(2,1)S(1)}, u32[]{:S(2)}, u32[]{:S(2)}) collective-permute-start(bf16[128,1536]{1,0:T(8,128)(2,1)S(1)} %subtract_convert_fusion.refs_2_), channel_id=1, source_target_pairs={{0,6},{1,7},{2,0},{3,1},{4,2},{5,3},{6,4},{7,5},{8,14},{9,15},{10,... | collective-permute-start | bytes 1179656 | tf_op jit(solution)/shard_map/ppermute | solution.py:20
  17.2 37.7 %collective-permute-start.15 = (bf16[128,1536]{1,0:T(8,128)(2,1)S(1)}, bf16[128,1536]{1,0:T(8,128)(2,1)S(1)}, u32[]{:S(2)}, u32[]{:S(2)}) collective-permute-start(bf16[128,1536]{1,0:T(8,128)(2,1)S(1)} %subtract_convert_fusion.refs_2_), channel_id=1, source_target_pairs={{0,4},{1,5},{2,6},{3,7},{4,0},{5,1},{6,2},{7,3},{8,12},{9,13},{10,... | collective-permute-start | bytes 1179656 | tf_op jit(solution)/shard_map/ppermute | solution.py:20
  19.3 35.6 %collective-permute-start.14 = (bf16[128,1536]{1,0:T(8,128)(2,1)S(1)}, bf16[128,1536]{1,0:T(8,128)(2,1)S(1)}, u32[]{:S(2)}, u32[]{:S(2)}) collective-permute-start(bf16[128,1536]{1,0:T(8,128)(2,1)S(1)} %subtract_convert_fusion.refs_2_), channel_id=1, source_target_pairs={{0,2},{1,3},{2,4},{3,5},{4,6},{5,7},{6,0},{7,1},{8,10},{9,11},{10,... | collective-permute-start | bytes 1179656 | tf_op jit(solution)/shard_map/ppermute | solution.py:20
  20.9 34.1 %collective-permute-start.13 = (bf16[128,1536]{1,0:T(8,128)(2,1)S(1)}, bf16[128,1536]{1,0:T(8,128)(2,1)S(1)}, u32[]{:S(2)}, u32[]{:S(2)}) collective-permute-start(bf16[128,1536]{1,0:T(8,128)(2,1)S(1)} %subtract_convert_fusion.refs_2_), channel_id=1, source_target_pairs={{0,1},{1,0},{2,3},{3,2},{4,5},{5,4},{6,7},{7,6},{8,9},{9,8},{10,11... | collective-permute-start | bytes 1179656 | tf_op jit(solution)/shard_map/ppermute | solution.py:20
  27.7 26.9 %all-to-all-start = ((bf16[256,2,384]{2,1,0:T(2,128)(2,1)}), bf16[256,2,384]{2,1,0:T(2,128)(2,1)S(1)}, u32[]{:S(2)}, u32[]{:S(2)}) async-start(bf16[256,2,384]{2,1,0:T(2,128)(2,1)} %copy.15), calls=%async_computation | async-start | bytes 786432 | tf_op jit(solution)/shard_map/cond/branch_1_fun/all_to_all | solution.py:197
  54.9 4.0 %copy-start.1 = (bf16[128,1536]{1,0:T(8,128)(2,1)}, bf16[128,1536]{1,0:T(8,128)(2,1)S(1)}, u32[]{:S(2)}) copy-start(bf16[128,1536]{1,0:T(8,128)(2,1)S(1)} %collective-permute-done.16.refs_5_) | copy-start | bytes 1179652
  54.9 4.0 %copy-start.2 = (bf16[128,1536]{1,0:T(8,128)(2,1)}, bf16[128,1536]{1,0:T(8,128)(2,1)S(1)}, u32[]{:S(2)}) copy-start(bf16[128,1536]{1,0:T(8,128)(2,1)S(1)} %collective-permute-done.15.refs_4_) | copy-start | bytes 1179652
  54.9 4.0 %copy-start.3 = (bf16[128,1536]{1,0:T(8,128)(2,1)}, bf16[128,1536]{1,0:T(8,128)(2,1)S(1)}, u32[]{:S(2)}) copy-start(bf16[128,1536]{1,0:T(8,128)(2,1)S(1)} %collective-permute-done.14.refs_3_) | copy-start | bytes 1179652
  54.9 4.0 %copy-start.4 = (bf16[128,1536]{1,0:T(8,128)(2,1)}, bf16[128,1536]{1,0:T(8,128)(2,1)S(1)}, u32[]{:S(2)}) copy-start(bf16[128,1536]{1,0:T(8,128)(2,1)S(1)} %collective-permute-done.13.refs_6_) | copy-start | bytes 1179652
  54.9 33.6 %collective-permute-start.19 = (bf16[128,1536]{1,0:T(8,128)(2,1)S(1)}, bf16[128,1536]{1,0:T(8,128)(2,1)S(1)}, u32[]{:S(2)}, u32[]{:S(2)}) collective-permute-start(bf16[128,1536]{1,0:T(8,128)(2,1)S(1)} %collective-permute-done.13.refs_6_), channel_id=1, source_target_pairs={{0,6},{1,7},{2,0},{3,1},{4,2},{5,3},{6,4},{7,5},{8,14},{9,15},{10,... | collective-permute-start | bytes 1179656 | tf_op jit(solution)/shard_map/ppermute | solution.py:20
  56.6 32.0 %collective-permute-start.18 = (bf16[128,1536]{1,0:T(8,128)(2,1)S(1)}, bf16[128,1536]{1,0:T(8,128)(2,1)S(1)}, u32[]{:S(2)}, u32[]{:S(2)}) collective-permute-start(bf16[128,1536]{1,0:T(8,128)(2,1)S(1)} %collective-permute-done.13.refs_6_), channel_id=1, source_target_pairs={{0,4},{1,5},{2,6},{3,7},{4,0},{5,1},{6,2},{7,3},{8,12},{9,13},{10,... | collective-permute-start | bytes 1179656 | tf_op jit(solution)/shard_map/ppermute | solution.py:20
  56.9 31.7 %collective-permute-start.17 = (bf16[128,1536]{1,0:T(8,128)(2,1)S(1)}, bf16[128,1536]{1,0:T(8,128)(2,1)}, u32[]{:S(2)}, u32[]{:S(2)}) collective-permute-start(bf16[128,1536]{1,0:T(8,128)(2,1)S(1)} %collective-permute-done.13.refs_6_), channel_id=1, source_target_pairs={{0,2},{1,3},{2,4},{3,5},{4,6},{5,7},{6,0},{7,1},{8,10},{9,11},{10,... | collective-permute-start | bytes 1179656 | tf_op jit(solution)/shard_map/ppermute | solution.py:20
  58.9 3.2 %collective-permute-start = (bf16[3,8,2,384]{3,1,2,0:T(8,128)(2,1)S(1)}, bf16[3,8,2,384]{3,1,2,0:T(8,128)(2,1)S(1)}, u32[]{:S(2)}, u32[]{:S(2)}) collective-permute-start(bf16[3,8,2,384]{3,1,2,0:T(8,128)(2,1)S(1)} %get-tuple-element.19), channel_id=1, source_target_pairs={{0,16},{8,24},{16,0},{24,8},{32,48},{40,56},{48,32},{56,40},{64,80... | collective-permute-start | bytes 110600 | tf_op jit(solution)/shard_map/cond/branch_1_fun/ppermute | solution.py:20
  62.1 4.7 %collective-permute-start.1 = (bf16[2,3,8,2,384]{4,2,3,1,0:T(8,128)(2,1)S(1)}, bf16[2,3,8,2,384]{4,2,3,1,0:T(8,128)(2,1)S(1)}, u32[]{:S(2)}, u32[]{:S(2)}) collective-permute-start(bf16[2,3,8,2,384]{4,2,3,1,0:T(8,128)(2,1)S(1)} %maximum_select_fusion.2), channel_id=1, source_target_pairs={{0,32},{8,40},{16,48},{24,56},{32,0},{40,8},{48,16},{56,24},{64,96... | collective-permute-start | bytes 221192 | tf_op jit(solution)/shard_map/cond/branch_1_fun/ppermute | solution.py:20
  66.8 4.5 %collective-permute-start.3 = (bf16[4,3,8,2,384]{4,2,3,1,0:T(8,128)(2,1)S(1)}, bf16[4,3,8,2,384]{4,2,3,1,0:T(8,128)(2,1)S(1)}, u32[]{:S(2)}, u32[]{:S(2)}) collective-permute-start(bf16[4,3,8,2,384]{4,2,3,1,0:T(8,128)(2,1)S(1)} %bitcast.32), channel_id=1, source_target_pairs={{0,192},{8,200},{16,208},{24,216},{32,224},{40,232},{48,240},{56,2... | collective-permute-start | bytes 442376 | tf_op jit(solution)/shard_map/cond/branch_1_fun/ppermute | solution.py:20
  67.8 4.4 %collective-permute-start.2 = (bf16[4,3,8,2,384]{4,2,3,1,0:T(8,128)(2,1)S(1)}, bf16[4,3,8,2,384]{4,2,3,1,0:T(8,128)(2,1)S(1)}, u32[]{:S(2)}, u32[]{:S(2)}) collective-permute-start(bf16[4,3,8,2,384]{4,2,3,1,0:T(8,128)(2,1)S(1)} %bitcast.33), channel_id=1, source_target_pairs={{0,64},{8,72},{16,80},{24,88},{32,96},{40,104},{48,112},{56,120},{... | collective-permute-start | bytes 442376 | tf_op jit(solution)/shard_map/cond/branch_1_fun/ppermute | solution.py:20
  72.2 5.9 %collective-permute-start.4 = (bf16[4,3,8,2,384]{4,2,3,1,0:T(8,128)(2,1)S(1)}, bf16[4,3,8,2,384]{4,2,3,1,0:T(8,128)(2,1)S(1)}, u32[]{:S(2)}, u32[]{:S(2)}) collective-permute-start(bf16[4,3,8,2,384]{4,2,3,1,0:T(8,128)(2,1)S(1)} %bitcast.34), channel_id=1, source_target_pairs={{0,128},{8,136},{16,144},{24,152},{32,160},{40,168},{48,176},{56,1... | collective-permute-start | bytes 442376 | tf_op jit(solution)/shard_map/cond/branch_1_fun/ppermute | solution.py:20
  79.7 8.9 %collective-permute-start.5 = (bf16[48,6144]{1,0:T(8,128)(2,1)}, bf16[48,6144]{1,0:T(8,128)(2,1)}, u32[]{:S(2)}, u32[]{:S(2)}) collective-permute-start(bf16[48,6144]{1,0:T(8,128)(2,1)} %reshape.100), channel_id=1, source_target_pairs={{0,8},{8,0},{16,24},{24,16},{32,40},{40,32},{48,56},{56,48},{64,72... | collective-permute-start | bytes 1769480 | tf_op jit(solution)/shard_map/cond/branch_1_fun/ppermute | solution.py:20
  88.6 0.7 copy-start.5
  88.6 0.9 copy-start.6
